TPU v7x, 32 devices: a whole 2x2x4 slice. The times are simulated.
32 devices in a mesh: ctx: 32 (over z, y, x, core), head: 1.
Axes of the slice: x: 2, y: 2, z: 4, core: 2. Of those that a mesh axis runs over, the one named last changes fastest.
Arguments:
- queries: bfloat16 [1, 12288, 128], P('head', 'ctx'), may hold values from -150 to 150
- keys: bfloat16 [1, 12288, 128], P('head', 'ctx'), may hold values from -8 to 8
- values: bfloat16 [1, 12288, 128], P('head', 'ctx'), may hold values from -6 to 6
- out_weight: bfloat16 [1, 128, 4096], P('head'), may hold values from -0.5 to 0.5
Outputs:
- projected: bfloat16 [12288, 4096], P('ctx', 'head')
All inputs are finite; a program needn't handle non-finite values.
Results may differ from a plain program's by a relative error of at most 0.012.
Values may be sent and summed in bfloat16 or wider, within the bound.
No kernel may reach another device: no remote copies, remote signals or barrier semaphores. Data moves between devices by JAX's collectives and lax.ppermute only.
A program may use at most 256 MiB of HBM per device.

v0:
```python
import math

import jax
import jax.numpy as jnp
from jax import lax
from jax.sharding import PartitionSpec as P

big_negative = -1e30


def empty_running(row_count, width):
    return (
        jnp.full((row_count,), big_negative, jnp.float32),
        jnp.zeros((row_count,), jnp.float32),
        jnp.zeros((row_count, width), jnp.float32),
    )


def attend(running, query_rows, query_pos, key_block, value_block, key_pos):
    row_max, row_total, summed = running
    scaling = 1.0 / math.sqrt(query_rows.shape[1])
    scores = (
        lax.dot_general(
            query_rows, key_block, (((1,), (1,)), ((), ())), preferred_element_type=jnp.float32
        )
        * scaling
    )
    scores = jnp.where(key_pos[None, :] <= query_pos[:, None], scores, jnp.float32(big_negative))
    new_max = jnp.maximum(row_max, jnp.max(scores, axis=1))
    exps = jnp.exp(scores - new_max[:, None])
    row_total = jnp.sum(exps, axis=1)
    summed = jnp.dot(exps.astype(jnp.bfloat16), value_block, preferred_element_type=jnp.float32)
    return (new_max, row_total, summed)


def maybe_attend(running, query_rows, query_pos, block_pair, first_row):
    key_pos = jnp.arange(block_pair.shape[1], dtype=jnp.int32)

    def taken(carried):
        return attend(carried, query_rows, query_pos, block_pair[0], block_pair[1], key_pos)

    def skipped(carried):
        return carried

    return lax.cond(first_row <= query_pos[-1], taken, skipped, running)


def finish(running):
    return (running[2] / running[1][:, None]).astype(jnp.bfloat16)


def per_device(queries, keys, values, out_weight):
    my_index = lax.axis_index("ctx")
    row_count = queries.shape[1]
    width = queries.shape[2]
    own_rows = queries[0]
    first_pos = my_index * row_count
    stacked = jnp.stack([keys[0], values[0]])
    query_pos = first_pos + jnp.arange(row_count, dtype=jnp.int32)
    start_state = empty_running(row_count, width)
    folded = maybe_attend(
        start_state,
        own_rows,
        query_pos,
        lax.all_gather(stacked, "ctx", axis=1, tiled=True),
        jnp.int32(0),
    )
    attention = finish(folded)
    partial_out = jnp.dot(attention, out_weight[0], preferred_element_type=jnp.float32)
    return lax.psum_scatter(
        partial_out.astype(jnp.bfloat16), "head", scatter_dimension=1, tiled=True
    )


def solution(mesh):
    placed = (
        P("head", "ctx", None),
        P("head", "ctx", None),
        P("head", "ctx", None),
        P("head", None, None),
    )
    return jax.shard_map(
        per_device, mesh=mesh, in_specs=placed, out_specs=P("ctx", "head"), check_vma=False
    )
```

profile of v0, /device:TPU:19, one launch (start us, length us, event | category | flops | bytes accessed | tf_op | source)
XLA Modules:
  0.0 115.2 jit_solution(5150048835803995417)
XLA Ops:
  6.5 0.0 copy-start
  6.5 0.0 all-gather.2.cloned.1.call-start
  6.5 1.7 %pad_maximum_fusion = bf16[2,384,128]{2,1,0:T(8,128)(2,1)} fusion(bf16[1,384,128]{2,1,0:T(8,128)(2,1)} %param.8, bf16[1,384,128]{2,1,0:T(8,128)(2,1)} %param.7), kind=kLoop, calls=%fused_computation.14 | loop fusion | flops 98304 | bytes 393216 | tf_op jit(solution)/shard_map/stack | solution.py:58
  8.3 0.0 all-gather.2.cloned.1.call-update
  8.3 0.6 slice.9
  9.6 71.0 %all-gather.2.cloned.1.call-done = bf16[2,12288,128]{2,1,0:T(8,128)(2,1)} async-done(((bf16[2,384,128]{2,1,0:T(8,128)(2,1)}), bf16[2,12288,128]{2,1,0:T(8,128)(2,1)}) %all-gather.2.cloned.1.call-update) | async-done | bytes 6291472 | tf_op jit(solution)/shard_map/all_gather | solution.py:65
  80.6 25.0 %conditional.1 = (f32[384]{0:T(512)S(1)}, f32[384,128]{1,0:T(8,128)S(1)}) conditional(s32[]{:T(128)} %bitcast.3, () %tuple.13, (s32[12288]{0:T(1024)S(1)}, s32[384]{0:T(512)S(1)}, bf16[1,384,128]{2,1,0:T(8,128)(2,1)}, bf16[2,12288,128]{2,1,0:T(8,128)(2,1)}) %tuple.14), branch_computations={%region_0.0_spmd, %region_1.4_spmd} | conditional | flops 2453667328 | bytes 138766896 | solution.py:45
  80.6 4.9 %fusion.12 = (f32[384]{0:T(512)S(1)}, f32[384,12288]{1,0:T(8,128)S(1)}) fusion(bf16[2,12288,128]{2,1,0:T(8,128)(2,1)} %get-tuple-element.17, bf16[1,384,128]{2,1,0:T(8,128)(2,1)} %get-tuple-element.23, s32[384]{0:T(512)S(1)} %get-tuple-element.15, s32[12288]{0:T(1024)S(1)} %get-tuple-element.14), kind=kOutput, calls=%fused_computation.18 | convolution fusion | flops 1226833536 | bytes 22170624 | tf_op jit(solution)/shard_map/cond/branch_1_fun/dot_general | solution.py:23
  85.5 0.0 copy-start.1
  85.5 6.4 %copy-done.1 = f32[384,12288]{1,0:T(8,128)} copy-done((f32[384,12288]{1,0:T(8,128)}, f32[384,12288]{1,0:T(8,128)S(1)}, u32[]{:S(2)}) %copy-start.1) | copy-done | bytes 18874392 | tf_op jit(solution)/shard_map/cond
  92.0 4.7 %fusion.2 = f32[384,128]{1,0:T(8,128)S(1)} fusion(f32[384,12288]{1,0:T(8,128)S(1)} %get-tuple-element.25, f32[384]{0:T(512)S(1)} %broadcast_maximum_fusion, bf16[2,12288,128]{2,1,0:T(8,128)(2,1)} %get-tuple-element.17), kind=kOutput, calls=%fused_computation.4 | convolution fusion | flops 1217396736 | bytes 22218240 | tf_op jit(solution)/shard_map/cond/branch_1_fun/dot_general | solution.py:32
  96.7 9.0 %fusion.1 = f32[384]{0:T(512)S(1)} fusion(f32[384,12288]{1,0:T(8,128)} %copy-done.1, f32[384]{0:T(512)S(1)} %broadcast_maximum_fusion), kind=kLoop, calls=%fused_computation.3 | loop fusion | flops 9436800 | bytes 18877440 | tf_op jit(solution)/shard_map/cond/branch_1_fun/reduce_sum | solution.py:31
  105.6 0.0 copy-done
  105.7 2.7 %convolution_convert_fusion = bf16[384,4096]{1,0:T(8,128)(2,1)} fusion(bf16[1,128,4096]{2,1,0:T(8,128)(2,1)S(1)} %copy-done, f32[384,128]{1,0:T(8,128)S(1)} %get-tuple-element.20, f32[384]{0:T(512)S(1)} %get-tuple-element.21), kind=kOutput, calls=%fused_computation.12 | convolution fusion | flops 404324352 | bytes 4392448 | tf_op jit(solution)/shard_map/dot_general | solution.py:69
  (3 shorter events, 0.0 us)
Async XLA Ops:
  6.5 99.1 %copy-start = (bf16[1,128,4096]{2,1,0:T(8,128)(2,1)S(1)}, bf16[1,128,4096]{2,1,0:T(8,128)(2,1)}, u32[]{:S(2)}) copy-start(bf16[1,128,4096]{2,1,0:T(8,128)(2,1)} %param.9) | copy-start | bytes 3145732
  6.5 74.1 %all-gather.2.cloned.1.call-start = ((), (), s32[]{:S(2)}) async-start(), calls=%async_computation | async-start | bytes 6488064 | tf_op jit(solution)/shard_map/all_gather | solution.py:65
  85.5 6.5 %copy-start.1 = (f32[384,12288]{1,0:T(8,128)}, f32[384,12288]{1,0:T(8,128)S(1)}, u32[]{:S(2)}) copy-start(f32[384,12288]{1,0:T(8,128)S(1)} %get-tuple-element.25) | copy-start | bytes 56623108 | tf_op jit(solution)/shard_map/cond
Sparse Core Ops, SparseCore 0:
  10.2 70.3 all-gather.1
where the time goes:
time: 117 us; the launch traced here: 115 us
  waiting for transfers between devices  71 us (61%)
  between operations  14 us (12%)
  matrix products  12.3 us (11%)
  other arithmetic  10.7 us (9%)
  local copies, waits for them, and re-layouts  7.09 us (6%)
    all_gather x1, waiting for transfers between devices, per_device(): lax.all_gather(stacked, 'ctx', axis=1, tiled=True)  71 us
    reduce_sum x1, other arithmetic, attend(): row_total = jnp.sum(exps, axis=1)  8.99 us
    cond x2, local copies, waits for them, and re-layouts  6.44 us
    dot_general x1, matrix products, attend(): lax.dot_general(query_rows, key_block, (((1,), (1,)), ((), ())), preferre...  4.9 us
    dot_general x1, matrix products, attend(): jnp.dot(exps.astype(jnp.bfloat16), value_block, preferred_element_type=jn...  4.66 us
    dot_general x1, matrix products, per_device(): jnp.dot(attention, out_weight[0], preferred_element_type=jnp.float32)  2.7 us
  transfers between devices with their start and end apart: 1, of which 1 were waited for; matrix products, arithmetic and copies ran while one was open for 1% of the time, Pallas kernels for 0%

commit v1 on v0

v1 whole, which is shorter than its diff:
```python
import functools
import math

import jax
import jax.numpy as jnp
from jax import lax
from jax.experimental import pallas as pl
from jax.experimental.pallas import tpu as pltpu
from jax.sharding import PartitionSpec as P

PLANES = 4
STAT_ROWS = 16
LEGS = {"a": 2, "b": 1, "c": 3}
NEGATIVE = -1e30
LOG2E = 1.4426950408889634


def dot_tn(a, b):
    return lax.dot_general(a, b, (((0,), (0,)), ((), ())), preferred_element_type=jnp.float32)


def dot_nt(a, b):
    return lax.dot_general(a, b, (((1,), (1,)), ((), ())), preferred_element_type=jnp.float32)


def advance(q, piece_refs, state, step, place=None):
    rows, width = q.shape
    length = piece_refs[0].shape[1]
    factor = LOG2E / math.sqrt(width)

    def scores_of(j):
        scores = dot_nt(jnp.concatenate([ref[0] for ref in piece_refs[j : j + step]], axis=0), q)
        if place is not None:
            index = lax.broadcasted_iota(jnp.int32, (length, 1), 0)
            key_pos = jnp.concatenate([(place ^ (j + i)) * length + index for i in range(step)], axis=0)
            query_pos = place * length + lax.broadcasted_iota(jnp.int32, (1, rows), 1)
            scores = jnp.where(key_pos <= query_pos, scores, NEGATIVE)
        return scores

    coming = scores_of(0)
    for j in range(0, len(piece_refs), step):
        scores = coming
        if j + step < len(piece_refs):
            coming = scores_of(j + step)
        v = jnp.concatenate([ref[1] for ref in piece_refs[j : j + step]], axis=0)
        top = jnp.max(scores, axis=0, keepdims=True)
        if state is not None:
            top = jnp.maximum(top, state[0])
        weights = jnp.exp2((scores - top) * factor)
        total = jnp.sum(weights, axis=0, keepdims=True)
        summed = dot_tn(v, weights.astype(jnp.bfloat16))
        if state is not None:
            kept = jnp.exp2((state[0] - top) * factor)
            total, summed = total + state[1] * kept, summed + state[2] * kept
        state = top, total, summed
    return state


def finish(state, width):
    top, total, summed = state
    return summed / total, top * (LOG2E / math.sqrt(width)) + jnp.log2(total)


def where_earlier(leg, group, body):
    plane = lax.axis_index("ctx") // group
    pl.when((plane ^ leg) > plane)(body)


def store_partial(out_ref, state, width):
    store_partial_of(out_ref, *finish(state, width), width)


def store_partial_of(out_ref, out, lse, width):
    out_ref[:width, :] = out.astype(jnp.bfloat16)
    high = lse.astype(jnp.bfloat16).astype(jnp.float32)
    middle = (lse - high).astype(jnp.bfloat16).astype(jnp.float32)
    low = lse - high - middle
    row = lax.broadcasted_iota(jnp.int32, (STAT_ROWS, 1), 0)
    stat = jnp.where(row == 0, high, jnp.where(row == 1, middle, jnp.where(row == 2, low, 0.0)))
    out_ref[width:, :] = stat.astype(jnp.bfloat16)


def remote_kernel(leg, group, q_ref, *refs):
    piece_refs, out_ref = refs[:-1], refs[-1]
    where_earlier(leg, group, lambda: store_partial(out_ref, advance(q_ref[...], piece_refs, None, 2), q_ref.shape[1]))


def load_partial(ref, width):
    stat = ref[width:, :].astype(jnp.float32)
    row = lax.broadcasted_iota(jnp.int32, (STAT_ROWS, 1), 0)
    return ref[:width, :].astype(jnp.float32), jnp.sum(jnp.where(row < 3, stat, 0.0), axis=0, keepdims=True)


def crossing_kernel(group, q_ref, *refs):
    piece_refs, out_ref = refs[:-1], refs[-1]
    width = q_ref.shape[1]

    def body():
        top, total, summed = advance(q_ref[...], piece_refs, None, 2)
        row = lax.broadcasted_iota(jnp.int32, (8, 1), 0)
        out_ref[:width, :] = summed
        out_ref[width:, :] = jnp.where(row == 0, top, total)

    where_earlier(LEGS["c"], group, body)


def join_kernel(group, state_ref, other_ref, out_ref):
    width = state_ref.shape[0] - 8

    def body():
        state = state_ref[width : width + 1, :], state_ref[width + 1 : width + 2, :], state_ref[:width, :]
        out, lse = finish(state, width)
        other_out, other_lse = load_partial(other_ref, width)
        top = jnp.maximum(lse, other_lse)
        share, other_share = jnp.exp2(lse - top), jnp.exp2(other_lse - top)
        store_partial_of(out_ref, *merged([out, other_out], [share, other_share], top), width)

    where_earlier(LEGS["c"], group, body)


def merged(parts, shares, top):
    total = functools.reduce(jnp.add, shares)
    summed = functools.reduce(jnp.add, [part * (share / total) for part, share in zip(parts, shares)])
    return summed, top + jnp.log2(total)


def own_kernel(group, q_ref, *refs):
    piece_refs, out_ref, lse_ref = refs[:-2], refs[-2], refs[-1]
    place = lax.rem(lax.axis_index("ctx"), group)
    out, lse = finish(advance(q_ref[...], piece_refs, None, 2, place), q_ref.shape[1])
    out_ref[...] = out
    lse_ref[...] = jnp.broadcast_to(lse, lse_ref.shape)


def merge_kernel(group, own_ref, lse_ref, c_ref, b_ref, w_ref, out_ref, attention_ref, tiles_ref, sems):
    width, rows = own_ref.shape
    plane = lax.axis_index("ctx") // group
    lses, parts = [lse_ref[:1, :]], [own_ref[...]]
    for leg, ref in (("c", c_ref), ("b", b_ref)):
        arrived = (plane ^ LEGS[leg]) < plane
        out, lse = load_partial(ref, width)
        lses.append(jnp.where(arrived, lse, NEGATIVE))
        parts.append(jnp.where(arrived, out, 0.0))
    top = functools.reduce(jnp.maximum, lses)
    attention, _ = merged(parts, [jnp.exp2(lse - top) for lse in lses], top)
    attention_ref[...] = jnp.transpose(attention).astype(jnp.bfloat16)
    copies = []
    block = tiles_ref.shape[2]
    for index in range(tiles_ref.shape[0]):
        for at in range(0, block, 256):
            columns = slice(index * block + at, index * block + at + 256)
            tiles_ref[index, :, at : at + 256] = jnp.dot(
                attention_ref[...], w_ref[:, columns], preferred_element_type=jnp.float32
            ).astype(jnp.bfloat16)
        columns = slice(index * block, (index + 1) * block)
        copies.append(pltpu.make_async_copy(tiles_ref.at[index], out_ref.at[:, columns], sems.at[index]))
        copies[-1].start()
    for copy in copies:
        copy.wait()


VMEM = pl.BlockSpec(memory_space=pltpu.VMEM)


def per_device(queries, keys, values, out_weight):
    count = lax.axis_size("ctx")
    group = count // PLANES
    own = queries[0]
    rows, width = own.shape
    columns = out_weight.shape[2]
    key_count = rows * group
    params = pltpu.CompilerParams(vmem_limit_bytes=24 * 1024 * 1024)
    cost = pl.CostEstimate(flops=4 * rows * key_count * width, bytes_accessed=4 * key_count * width, transcendentals=rows * key_count)

    def below(array):
        return lax.ppermute(
            array, "ctx", [(i, i ^ group if i < 2 * group else i ^ 1) for i in range(count)]
        )

    def across(mask, array):
        return lax.ppermute(array, "ctx", [(i, i ^ mask) for i in range(count)])

    k, v, _ = lax.optimization_barrier((keys[0], values[0], own))
    stacked = jnp.stack([k, v])
    pieces = {0: stacked}
    far = group - 2
    held, held_own = stacked, own
    from_two = across(2 * group, own)
    pieces[far] = across(far, stacked)
    pieces[1] = across(1, stacked)
    held, held_own, pieces[1] = lax.optimization_barrier((stacked, own, pieces[1]))
    for mask in range(far - 2, 0, -2):
        pieces[mask] = across(mask, held)
    from_one = across(group, held_own)
    passed = below(from_two)
    waits = {6: from_two, 4: from_one}
    for mask in range(2, group, 2):
        if mask in waits:
            pieces[mask], _ = lax.optimization_barrier((pieces[mask], waits[mask]))
        pieces[mask + 1] = across(1, pieces[mask])
    pieces = [pieces[j] for j in range(group)]

    partial = jax.ShapeDtypeStruct((width + STAT_ROWS, rows), jnp.bfloat16)

    def on_vmem(kernel, shape, count, name, cost):
        return pl.pallas_call(
            kernel,
            out_shape=shape,
            in_specs=[VMEM] * count,
            out_specs=VMEM,
            compiler_params=params,
            cost_estimate=cost,
            name=name,
        )

    small = pl.CostEstimate(flops=rows * width, bytes_accessed=rows * width, transcendentals=0)
    part_a = on_vmem(functools.partial(remote_kernel, LEGS["a"], group), partial, 1 + group, "remote_a", cost)(
        from_two, *pieces
    )
    swapped = below(part_a)
    state_c = on_vmem(
        functools.partial(crossing_kernel, group),
        jax.ShapeDtypeStruct((width + 8, rows), jnp.float32),
        1 + group,
        "remote_c",
        cost,
    )(passed, *pieces)
    joined = on_vmem(functools.partial(join_kernel, group), partial, 2, "join", small)(state_c, swapped)
    step = LEGS["c"] * group
    received_c = lax.ppermute(joined, "ctx", [(i, i ^ step) for i in range(2 * group)])
    part_b = on_vmem(functools.partial(remote_kernel, LEGS["b"], group), partial, 1 + group, "remote_b", cost)(
        from_one, *pieces
    )
    received_b = across(LEGS["b"] * group, part_b)

    own_part, own_lse = pl.pallas_call(
        functools.partial(own_kernel, group),
        out_shape=[jax.ShapeDtypeStruct((height, rows), jnp.float32) for height in (width, 8)],
        in_specs=[VMEM] * (1 + group),
        out_specs=[VMEM, VMEM],
        compiler_params=params,
        cost_estimate=cost,
        name="own",
    )(own, *pieces)

    partial_out = pl.pallas_call(
        functools.partial(merge_kernel, group),
        out_shape=jax.ShapeDtypeStruct((rows, columns), jnp.bfloat16),
        in_specs=[VMEM] * 5,
        out_specs=pl.BlockSpec(memory_space=pl.ANY),
        scratch_shapes=[
            pltpu.VMEM((rows, width), jnp.bfloat16),
            pltpu.VMEM((8, rows, columns // 8), jnp.bfloat16),
            pltpu.SemaphoreType.DMA((8,)),
        ],
        compiler_params=params,
        cost_estimate=pl.CostEstimate(
            flops=2 * rows * width * columns, bytes_accessed=2 * (rows + width) * columns, transcendentals=0
        ),
        name="merge",
    )(own_part, own_lse, received_c, received_b, out_weight[0])
    return lax.psum_scatter(partial_out, "head", scatter_dimension=1, tiled=True)


def solution(mesh):
    placed = (
        P("head", "ctx", None),
        P("head", "ctx", None),
        P("head", "ctx", None),
        P("head", None, None),
    )
    return jax.shard_map(
        per_device, mesh=mesh, in_specs=placed, out_specs=P("ctx", "head"), check_vma=False
    )
```

time: 117 us -> 32.3 us (0.28); the launches traced: 115 us -> 32.2 us
  waiting for transfers between devices: 71 us -> 14.9 us
  between operations: 14 us -> 0.09 us
  matrix products: 12.3 us -> 0 us
  starting transfers between devices: 0.01 us -> 10.1 us
  other arithmetic: 10.7 us -> 0.96 us
  local copies, waits for them, and re-layouts: 7.09 us -> 0.01 us
  Pallas kernels: 0 us -> 6.12 us
    all_gather x1 -> x0, waiting for transfers between devices: 71 us -> none  [per_device(): lax.all_gather(stacked, 'ctx', axis=1, tiled=True)]
    ppermute x0 -> x13, waiting for transfers between devices: none -> 14.9 us  [the longest x1 7.77 us: per_device(): lax.ppermute(joined, 'ctx', [(i, i ^ step) for i in range(2 * group)])]
    dot_general x3 -> x0, matrix products: 12.3 us -> none  [the longest x1 4.9 us: attend(): lax.dot_general(query_rows, key_block, (((1,), (1,)), ((), ())), preferre...]
    ppermute x0 -> x13, starting transfers between devices: none -> 10.1 us  [the longest x10 8.14 us: across(): return lax.ppermute(array, 'ctx', [(i, i ^ mask) for i in range(count)])]
    reduce_sum x1 -> x0, other arithmetic: 8.99 us -> none  [attend(): row_total = jnp.sum(exps, axis=1)]
    cond x2 -> x0, local copies, waits for them, and re-layouts: 6.44 us -> none
    pallas_call x0 -> x6, Pallas kernels: none -> 6.12 us  [the longest x1 2.1 us: per_device(): pl.pallas_call(functools.partial(merge_kernel, group), out_shape=jax.Shap...]
  transfers between devices with their start and end apart: 1 -> 13, of which waited for: 1 -> 6; matrix products, arithmetic and copies ran while one was open for 1% -> 0% of each run, Pallas kernels for 0% -> 12%
where the time goes in v1:
time: 32.3 us; the launch traced here: 32.2 us
  waiting for transfers between devices  14.9 us (46%)
  starting transfers between devices  10.1 us (31%)
  Pallas kernels  6.12 us (19%)
  other arithmetic  0.96 us (3%)
    ppermute x10, starting transfers between devices, across(): return lax.ppermute(array, 'ctx', [(i, i ^ mask) for i in range(count)])  8.14 us
    ppermute x1, waiting for transfers between devices, per_device(): lax.ppermute(joined, 'ctx', [(i, i ^ step) for i in range(2 * group)])  7.77 us
    ppermute x10, waiting for transfers between devices, across(): return lax.ppermute(array, 'ctx', [(i, i ^ mask) for i in range(count)])  7.08 us
    pallas_call x1, Pallas kernels, per_device(): pl.pallas_call(functools.partial(merge_kernel, group), out_shape=jax.Shap...  2.1 us
    pallas_call x1, Pallas kernels, per_device(): pl.pallas_call(functools.partial(own_kernel, group), out_shape=[jax.Shape...  2.09 us
    pallas_call x1, Pallas kernels, per_device(): on_vmem(functools.partial(remote_kernel, LEGS['b'], group), partial, 1 +...  1.89 us
    ppermute x1, starting transfers between devices, per_device(): lax.ppermute(joined, 'ctx', [(i, i ^ step) for i in range(2 * group)])  1.29 us
    another operation x1, other arithmetic, per_device(): stacked = jnp.stack([k, v])  0.96 us
  transfers between devices with their start and end apart: 13, of which 6 were waited for; matrix products, arithmetic and copies ran while one was open for 0% of the time, Pallas kernels for 12%

profile of v1, /device:TPU:19, one launch (start us, length us, event | category | flops | bytes accessed | tf_op | source)
XLA Modules:
  0.0 32.2 jit_solution(16044328030412292083)
XLA Ops:
  0.0 1.0 %pad_maximum_fusion.refs_0_ = bf16[2,384,128]{2,1,0:T(8,128)(2,1)S(1)} fusion(bf16[1,384,128]{2,1,0:T(8,128)(2,1)} %param.6, bf16[1,384,128]{2,1,0:T(8,128)(2,1)} %param.5), kind=kLoop, calls=%fused_computation | loop fusion | flops 98304 | bytes 393216 | tf_op jit(solution)/shard_map/stack | solution.py:184
  1.0 0.0 copy-start.1
  1.0 0.7 %collective-permute-start = (bf16[2,384,128]{2,1,0:T(8,128)(2,1)S(1)}, bf16[2,384,128]{2,1,0:T(8,128)(2,1)S(1)}, u32[]{:S(2)}, u32[]{:S(2)}) collective-permute-start(bf16[2,384,128]{2,1,0:T(8,128)(2,1)S(1)} %pad_maximum_fusion.refs_0_), channel_id=1, source_target_pairs={{0,1},{1,0},{2,3},{3,2},{4,5},{5,4},{6,7},{7,6},{8,9},{9,8},{10,11... | collective-permute-start | bytes 589832 | tf_op jit(solution)/shard_map/ppermute | solution.py:181
  1.7 1.2 %collective-permute-start.6 = (bf16[2,384,128]{2,1,0:T(8,128)(2,1)S(1)}, bf16[2,384,128]{2,1,0:T(8,128)(2,1)S(1)}, u32[]{:S(2)}, u32[]{:S(2)}) collective-permute-start(bf16[2,384,128]{2,1,0:T(8,128)(2,1)S(1)} %pad_maximum_fusion.refs_0_), channel_id=1, source_target_pairs={{0,6},{1,7},{2,4},{3,5},{4,2},{5,3},{6,0},{7,1},{8,14},{9,15},{10,... | collective-permute-start | bytes 589832 | tf_op jit(solution)/shard_map/ppermute | solution.py:181
  2.9 1.1 %collective-permute-start.3 = (bf16[2,384,128]{2,1,0:T(8,128)(2,1)S(1)}, bf16[2,384,128]{2,1,0:T(8,128)(2,1)S(1)}, u32[]{:S(2)}, u32[]{:S(2)}) collective-permute-start(bf16[2,384,128]{2,1,0:T(8,128)(2,1)S(1)} %pad_maximum_fusion.refs_0_), channel_id=1, source_target_pairs={{0,4},{1,5},{2,6},{3,7},{4,0},{5,1},{6,2},{7,3},{8,12},{9,13},{10,... | collective-permute-start | bytes 589832 | tf_op jit(solution)/shard_map/ppermute | solution.py:181
  4.0 0.4 %collective-permute-start.1 = (bf16[2,384,128]{2,1,0:T(8,128)(2,1)S(1)}, bf16[2,384,128]{2,1,0:T(8,128)(2,1)S(1)}, u32[]{:S(2)}, u32[]{:S(2)}) collective-permute-start(bf16[2,384,128]{2,1,0:T(8,128)(2,1)S(1)} %pad_maximum_fusion.refs_0_), channel_id=1, source_target_pairs={{0,2},{1,3},{2,0},{3,1},{4,6},{5,7},{6,4},{7,5},{8,10},{9,11},{10,... | collective-permute-start | bytes 589832 | tf_op jit(solution)/shard_map/ppermute | solution.py:181
  4.4 0.1 collective-permute-start.7
  4.4 1.3 %collective-permute-start.4 = (bf16[384,128]{1,0:T(8,128)(2,1)}, bf16[384,128]{1,0:T(8,128)(2,1)S(1)}, u32[]{:S(2)}, u32[]{:S(2)}) collective-permute-start(bf16[384,128]{1,0:T(8,128)(2,1)} %bitcast.8), channel_id=1, source_target_pairs={{0,8},{1,9},{2,10},{3,11},{4,12},{5,13},{6,14},{7,15},{8,0},{9,1},... | collective-permute-start | bytes 294920 | tf_op jit(solution)/shard_map/ppermute | solution.py:181
  5.7 3.5 %collective-permute-done.7.q_ref = bf16[384,128]{1,0:T(8,128)(2,1)S(1)} collective-permute-done((bf16[384,128]{1,0:T(8,128)(2,1)}, bf16[384,128]{1,0:T(8,128)(2,1)S(1)}, u32[]{:S(2)}, u32[]{:S(2)}) %collective-permute-start.7) | collective-permute-done | bytes 98336 | tf_op jit(solution)/shard_map/ppermute | solution.py:181
  9.3 2.7 %collective-permute-start.8 = (bf16[2,384,128]{2,1,0:T(8,128)(2,1)S(1)}, bf16[2,384,128]{2,1,0:T(8,128)(2,1)S(1)}, u32[]{:S(2)}, u32[]{:S(2)}) collective-permute-start(bf16[2,384,128]{2,1,0:T(8,128)(2,1)S(1)} %collective-permute-done.6.refs_6_), channel_id=1, source_target_pairs={{0,1},{1,0},{2,3},{3,2},{4,5},{5,4},{6,7},{7,6},{8,9},{9,8},{10,11... | collective-permute-start | bytes 589832 | tf_op jit(solution)/shard_map/ppermute | solution.py:181
  12.0 1.7 %collective-permute-done.3.refs_4_ = bf16[2,384,128]{2,1,0:T(8,128)(2,1)S(1)} collective-permute-done((bf16[2,384,128]{2,1,0:T(8,128)(2,1)S(1)}, bf16[2,384,128]{2,1,0:T(8,128)(2,1)S(1)}, u32[]{:S(2)}, u32[]{:S(2)}) %collective-permute-start.3) | collective-permute-done | bytes 196640 | tf_op jit(solution)/shard_map/ppermute | solution.py:181
  13.7 0.5 %collective-permute-start.5 = (bf16[2,384,128]{2,1,0:T(8,128)(2,1)S(1)}, bf16[2,384,128]{2,1,0:T(8,128)(2,1)S(1)}, u32[]{:S(2)}, u32[]{:S(2)}) collective-permute-start(bf16[2,384,128]{2,1,0:T(8,128)(2,1)S(1)} %collective-permute-done.3.refs_4_), channel_id=1, source_target_pairs={{0,1},{1,0},{2,3},{3,2},{4,5},{5,4},{6,7},{7,6},{8,9},{9,8},{10,11... | collective-permute-start | bytes 589832 | tf_op jit(solution)/shard_map/ppermute | solution.py:181
  14.2 0.1 collective-permute-start.2
  14.3 0.4 %collective-permute-start.9 = (bf16[384,128]{1,0:T(8,128)(2,1)S(1)}, bf16[384,128]{1,0:T(8,128)(2,1)S(1)}, u32[]{:S(2)}, u32[]{:S(2)}) collective-permute-start(bf16[384,128]{1,0:T(8,128)(2,1)S(1)} %collective-permute-done.7.q_ref), channel_id=1, source_target_pairs={{0,8},{1,9},{2,10},{3,11},{4,12},{5,13},{6,14},{7,15},{8,0},{9,1},... | collective-permute-start | bytes 294920 | tf_op jit(solution)/shard_map/ppermute | solution.py:176
  14.7 0.6 %collective-permute-done.5.refs_5_ = bf16[2,384,128]{2,1,0:T(8,128)(2,1)S(1)} collective-permute-done((bf16[2,384,128]{2,1,0:T(8,128)(2,1)S(1)}, bf16[2,384,128]{2,1,0:T(8,128)(2,1)S(1)}, u32[]{:S(2)}, u32[]{:S(2)}) %collective-permute-start.5) | collective-permute-done | bytes 196640 | tf_op jit(solution)/shard_map/ppermute | solution.py:181
  15.2 0.4 %collective-permute-done.2.refs_3_ = bf16[2,384,128]{2,1,0:T(8,128)(2,1)S(1)} collective-permute-done((bf16[2,384,128]{2,1,0:T(8,128)(2,1)S(1)}, bf16[2,384,128]{2,1,0:T(8,128)(2,1)S(1)}, u32[]{:S(2)}, u32[]{:S(2)}) %collective-permute-start.2) | collective-permute-done | bytes 196640 | tf_op jit(solution)/shard_map/ppermute | solution.py:181
  15.6 0.3 collective-permute-start.10
  15.9 1.9 %remote_b.1 = bf16[144,384]{1,0:T(8,128)(2,1)S(1)} custom-call(bf16[384,128]{1,0:T(8,128)(2,1)S(1)} %collective-permute-done.4.q_ref, bf16[2,384,128]{2,1,0:T(8,128)(2,1)S(1)} %pad_maximum_fusion.refs_0_, bf16[2,384,128]{2,1,0:T(8,128)(2,1)S(1)} %collective-permute-done.refs_1_, bf16[2,384,128]{2,1,0:T(8,128)(2,1)S(1)} %collective-permute-done.1.refs_2_, ...), custom_call_target="tpu_custom_call" | custom-call | flops 603979776 | bytes 1572864 | tf_op jit(solution)/shard_map/remote_b/pallas_call | solution.py:231
  17.8 0.1 collective-permute-start.12
  17.9 1.3 %collective-permute-start.11 = (bf16[144,384]{1,0:T(8,128)(2,1)S(1)}, bf16[144,384]{1,0:T(8,128)(2,1)S(1)}, u32[]{:S(2)}, u32[]{:S(2)}) collective-permute-start(bf16[144,384]{1,0:T(8,128)(2,1)S(1)} %join.1), channel_id=1, source_target_pairs={{0,24},{1,25},{2,26},{3,27},{4,28},{5,29},{6,30},{7,31},{8,16},{9,... | collective-permute-start | bytes 331784 | tf_op jit(solution)/shard_map/ppermute | solution.py:230
  19.2 2.1 %own.1 = (f32[128,384]{1,0:T(8,128)S(1)}, f32[8,384]{1,0:T(8,128)S(1)}) custom-call(bf16[384,128]{1,0:T(8,128)(2,1)S(1)} %bitcast.9, bf16[2,384,128]{2,1,0:T(8,128)(2,1)S(1)} %pad_maximum_fusion.refs_0_, bf16[2,384,128]{2,1,0:T(8,128)(2,1)S(1)} %collective-permute-done.refs_1_, bf16[2,384,128]{2,1,0:T(8,128)(2,1)S(1)} %collective-permute-done.1.refs_2_, ...), custom_call_target="tpu_custom_call" | custom-call | flops 603979776 | bytes 1572864 | tf_op jit(solution)/shard_map/own/pallas_call | solution.py:236
  21.3 0.9 %collective-permute-done.12.b_ref = bf16[144,384]{1,0:T(8,128)(2,1)S(1)} collective-permute-done((bf16[144,384]{1,0:T(8,128)(2,1)S(1)}, bf16[144,384]{1,0:T(8,128)(2,1)S(1)}, u32[]{:S(2)}, u32[]{:S(2)}) %collective-permute-start.12) | collective-permute-done | bytes 110624 | tf_op jit(solution)/shard_map/ppermute | solution.py:181
  22.3 7.8 %collective-permute-done.11.c_ref = bf16[144,384]{1,0:T(8,128)(2,1)S(1)} collective-permute-done((bf16[144,384]{1,0:T(8,128)(2,1)S(1)}, bf16[144,384]{1,0:T(8,128)(2,1)S(1)}, u32[]{:S(2)}, u32[]{:S(2)}) %collective-permute-start.11) | collective-permute-done | bytes 110624 | tf_op jit(solution)/shard_map/ppermute | solution.py:230
  30.1 2.1 %merge.1 = bf16[384,4096]{1,0:T(8,128)(2,1)} custom-call(f32[128,384]{1,0:T(8,128)S(1)} %get-tuple-element.21.own_ref, f32[8,384]{1,0:T(8,128)S(1)} %get-tuple-element.22.lse_ref, bf16[144,384]{1,0:T(8,128)(2,1)S(1)} %collective-permute-done.11.c_ref, bf16[144,384]{1,0:T(8,128)(2,1)S(1)} %collective-permute-done.12.b_ref, bf16[128,4096]{1,0:T(8,128)(2,1)S(1)} %bitcast.6), custom_call_target="tpu_custom_call" | custom-call | flops 402653184 | bytes 4194304 | tf_op jit(solution)/shard_map/merge/pallas_call | solution.py:246
  (13 shorter events, 0.1 us)
Async XLA Ops:
  1.0 18.3 %copy-start.1 = (bf16[1,384,128]{2,1,0:T(8,128)(2,1)S(1)}, bf16[1,384,128]{2,1,0:T(8,128)(2,1)}, u32[]{:S(2)}) copy-start(bf16[1,384,128]{2,1,0:T(8,128)(2,1)} %param.4) | copy-start | bytes 294916
  1.0 2.0 %collective-permute-start = (bf16[2,384,128]{2,1,0:T(8,128)(2,1)S(1)}, bf16[2,384,128]{2,1,0:T(8,128)(2,1)S(1)}, u32[]{:S(2)}, u32[]{:S(2)}) collective-permute-start(bf16[2,384,128]{2,1,0:T(8,128)(2,1)S(1)} %pad_maximum_fusion.refs_0_), channel_id=1, source_target_pairs={{0,1},{1,0},{2,3},{3,2},{4,5},{5,4},{6,7},{7,6},{8,9},{9,8},{10,11... | collective-permute-start | bytes 589832 | tf_op jit(solution)/shard_map/ppermute | solution.py:181
  1.7 7.5 %collective-permute-start.6 = (bf16[2,384,128]{2,1,0:T(8,128)(2,1)S(1)}, bf16[2,384,128]{2,1,0:T(8,128)(2,1)S(1)}, u32[]{:S(2)}, u32[]{:S(2)}) collective-permute-start(bf16[2,384,128]{2,1,0:T(8,128)(2,1)S(1)} %pad_maximum_fusion.refs_0_), channel_id=1, source_target_pairs={{0,6},{1,7},{2,4},{3,5},{4,2},{5,3},{6,0},{7,1},{8,14},{9,15},{10,... | collective-permute-start | bytes 589832 | tf_op jit(solution)/shard_map/ppermute | solution.py:181
  2.9 10.7 %collective-permute-start.3 = (bf16[2,384,128]{2,1,0:T(8,128)(2,1)S(1)}, bf16[2,384,128]{2,1,0:T(8,128)(2,1)S(1)}, u32[]{:S(2)}, u32[]{:S(2)}) collective-permute-start(bf16[2,384,128]{2,1,0:T(8,128)(2,1)S(1)} %pad_maximum_fusion.refs_0_), channel_id=1, source_target_pairs={{0,4},{1,5},{2,6},{3,7},{4,0},{5,1},{6,2},{7,3},{8,12},{9,13},{10,... | collective-permute-start | bytes 589832 | tf_op jit(solution)/shard_map/ppermute | solution.py:181
  4.0 10.1 %collective-permute-start.1 = (bf16[2,384,128]{2,1,0:T(8,128)(2,1)S(1)}, bf16[2,384,128]{2,1,0:T(8,128)(2,1)S(1)}, u32[]{:S(2)}, u32[]{:S(2)}) collective-permute-start(bf16[2,384,128]{2,1,0:T(8,128)(2,1)S(1)} %pad_maximum_fusion.refs_0_), channel_id=1, source_target_pairs={{0,2},{1,3},{2,0},{3,1},{4,6},{5,7},{6,4},{7,5},{8,10},{9,11},{10,... | collective-permute-start | bytes 589832 | tf_op jit(solution)/shard_map/ppermute | solution.py:181
  4.4 4.9 %collective-permute-start.7 = (bf16[384,128]{1,0:T(8,128)(2,1)}, bf16[384,128]{1,0:T(8,128)(2,1)S(1)}, u32[]{:S(2)}, u32[]{:S(2)}) collective-permute-start(bf16[384,128]{1,0:T(8,128)(2,1)} %bitcast.7), channel_id=1, source_target_pairs={{0,16},{1,17},{2,18},{3,19},{4,20},{5,21},{6,22},{7,23},{8,24},{9,... | collective-permute-start | bytes 294920 | tf_op jit(solution)/shard_map/ppermute | solution.py:181
  4.4 7.6 %collective-permute-start.4 = (bf16[384,128]{1,0:T(8,128)(2,1)}, bf16[384,128]{1,0:T(8,128)(2,1)S(1)}, u32[]{:S(2)}, u32[]{:S(2)}) collective-permute-start(bf16[384,128]{1,0:T(8,128)(2,1)} %bitcast.8), channel_id=1, source_target_pairs={{0,8},{1,9},{2,10},{3,11},{4,12},{5,13},{6,14},{7,15},{8,0},{9,1},... | collective-permute-start | bytes 294920 | tf_op jit(solution)/shard_map/ppermute | solution.py:181
  9.3 5.4 %collective-permute-start.8 = (bf16[2,384,128]{2,1,0:T(8,128)(2,1)S(1)}, bf16[2,384,128]{2,1,0:T(8,128)(2,1)S(1)}, u32[]{:S(2)}, u32[]{:S(2)}) collective-permute-start(bf16[2,384,128]{2,1,0:T(8,128)(2,1)S(1)} %collective-permute-done.6.refs_6_), channel_id=1, source_target_pairs={{0,1},{1,0},{2,3},{3,2},{4,5},{5,4},{6,7},{7,6},{8,9},{9,8},{10,11... | collective-permute-start | bytes 589832 | tf_op jit(solution)/shard_map/ppermute | solution.py:181
  13.7 1.5 %collective-permute-start.5 = (bf16[2,384,128]{2,1,0:T(8,128)(2,1)S(1)}, bf16[2,384,128]{2,1,0:T(8,128)(2,1)S(1)}, u32[]{:S(2)}, u32[]{:S(2)}) collective-permute-start(bf16[2,384,128]{2,1,0:T(8,128)(2,1)S(1)} %collective-permute-done.3.refs_4_), channel_id=1, source_target_pairs={{0,1},{1,0},{2,3},{3,2},{4,5},{5,4},{6,7},{7,6},{8,9},{9,8},{10,11... | collective-permute-start | bytes 589832 | tf_op jit(solution)/shard_map/ppermute | solution.py:181
  14.2 1.4 %collective-permute-start.2 = (bf16[2,384,128]{2,1,0:T(8,128)(2,1)S(1)}, bf16[2,384,128]{2,1,0:T(8,128)(2,1)S(1)}, u32[]{:S(2)}, u32[]{:S(2)}) collective-permute-start(bf16[2,384,128]{2,1,0:T(8,128)(2,1)S(1)} %collective-permute-done.1.refs_2_), channel_id=1, source_target_pairs={{0,1},{1,0},{2,3},{3,2},{4,5},{5,4},{6,7},{7,6},{8,9},{9,8},{10,11... | collective-permute-start | bytes 589832 | tf_op jit(solution)/shard_map/ppermute | solution.py:181
  14.3 3.6 %collective-permute-start.9 = (bf16[384,128]{1,0:T(8,128)(2,1)S(1)}, bf16[384,128]{1,0:T(8,128)(2,1)S(1)}, u32[]{:S(2)}, u32[]{:S(2)}) collective-permute-start(bf16[384,128]{1,0:T(8,128)(2,1)S(1)} %collective-permute-done.7.q_ref), channel_id=1, source_target_pairs={{0,8},{1,9},{2,10},{3,11},{4,12},{5,13},{6,14},{7,15},{8,0},{9,1},... | collective-permute-start | bytes 294920 | tf_op jit(solution)/shard_map/ppermute | solution.py:176
  15.6 14.5 %copy-start = (bf16[1,128,4096]{2,1,0:T(8,128)(2,1)S(1)}, bf16[1,128,4096]{2,1,0:T(8,128)(2,1)}, u32[]{:S(2)}) copy-start(bf16[1,128,4096]{2,1,0:T(8,128)(2,1)} %param.7) | copy-start | bytes 3145732
  15.6 2.3 %collective-permute-start.10 = (bf16[144,384]{1,0:T(8,128)(2,1)S(1)}, bf16[144,384]{1,0:T(8,128)(2,1)S(1)}, u32[]{:S(2)}, u32[]{:S(2)}) collective-permute-start(bf16[144,384]{1,0:T(8,128)(2,1)S(1)} %remote_a.1), channel_id=1, source_target_pairs={{0,8},{1,9},{2,10},{3,11},{4,12},{5,13},{6,14},{7,15},{8,0},{9,1},... | collective-permute-start | bytes 331784 | tf_op jit(solution)/shard_map/ppermute | solution.py:176
  17.8 4.5 %collective-permute-start.12 = (bf16[144,384]{1,0:T(8,128)(2,1)S(1)}, bf16[144,384]{1,0:T(8,128)(2,1)S(1)}, u32[]{:S(2)}, u32[]{:S(2)}) collective-permute-start(bf16[144,384]{1,0:T(8,128)(2,1)S(1)} %remote_b.1), channel_id=1, source_target_pairs={{0,8},{1,9},{2,10},{3,11},{4,12},{5,13},{6,14},{7,15},{8,0},{9,1},... | collective-permute-start | bytes 331784 | tf_op jit(solution)/shard_map/ppermute | solution.py:181
  17.9 12.1 %collective-permute-start.11 = (bf16[144,384]{1,0:T(8,128)(2,1)S(1)}, bf16[144,384]{1,0:T(8,128)(2,1)S(1)}, u32[]{:S(2)}, u32[]{:S(2)}) collective-permute-start(bf16[144,384]{1,0:T(8,128)(2,1)S(1)} %join.1), channel_id=1, source_target_pairs={{0,24},{1,25},{2,26},{3,27},{4,28},{5,29},{6,30},{7,31},{8,16},{9,... | collective-permute-start | bytes 331784 | tf_op jit(solution)/shard_map/ppermute | solution.py:230
